TPU v7x, 256 devices: a whole 4x4x8 slice. The times are simulated.
256 devices in a mesh: ctx: 128 (over x, z, y_hi, core), ch: 2 (over y_lo).
Axes of the slice: x: 4, y: 4 (y_hi: 2, y_lo: 2; y = y_hi * 2 + y_lo), z: 8, core: 2. Of those that a mesh axis runs over, the one named last changes fastest.
Arguments:
- queries: bfloat16 [32768, 4096], P('ctx', 'ch'), may hold values from -6 to 6
- keys: bfloat16 [32768, 4096], P('ctx', 'ch'), may hold values from -6 to 6
- values: bfloat16 [32768, 4096], P('ctx', 'ch'), may hold values from -6 to 6
- grad_out: bfloat16 [32768, 4096], P('ctx', 'ch'), may hold values from -0.0009765625 to 0.0009765625
Outputs:
- filter_grad: float32 [4, 1024], P('ch')
All inputs are finite; a program needn't handle non-finite values.
Results may differ from a plain program's by a relative error of at most 0.004.
Values may be sent and summed in bfloat16 or wider, within the bound.
No kernel may reach another device: no remote copies, remote signals or barrier semaphores. Data moves between devices by JAX's collectives and lax.ppermute only.
A program may use at most 64 MiB of HBM per device.

v0:
```python
import jax
import jax.numpy as jnp
from jax import lax
from jax.sharding import PartitionSpec as P

GROUP_CH = 1024
HOPS = 4


def from_behind(shard, axis, by):
    peers = lax.axis_size(axis)
    pairs = [(i, i + by) for i in range(peers) if 0 <= i + by < peers]
    return lax.ppermute(shard, axis, pairs)


def lag_sums(product):
    count = product.shape[0]
    tok_rows = product.shape[1]
    padded = jnp.pad(product, ((0, 0), (0, 0), (0, tok_rows)))
    flat = padded.reshape(count, tok_rows * 2 * tok_rows)[:, : tok_rows * (2 * tok_rows - 1)]
    return jnp.sum(flat.reshape(count, tok_rows, 2 * tok_rows - 1), axis=1)


def on_device(queries, keys, values, grad_out):
    mixed = (keys.astype(jnp.float32) * values.astype(jnp.float32)).astype(jnp.bfloat16)
    weighted = (queries.astype(jnp.float32) * grad_out.astype(jnp.float32)).astype(jnp.bfloat16)
    tok_rows = mixed.shape[0]
    groups_here = mixed.shape[1] // GROUP_CH
    blocks = [mixed]
    for offset in range(HOPS):
        blocks.append(from_behind(blocks[-1], "ctx", 1))
    target_rows = weighted.reshape(tok_rows, groups_here, GROUP_CH)
    totals = jnp.zeros((groups_here, (HOPS + 2) * tok_rows), jnp.float32)
    for distance in range(HOPS + 1):
        flipped = blocks[distance][::-1].reshape(tok_rows, groups_here, GROUP_CH)
        product = jnp.einsum(
            "tgc,sgc->gts", target_rows, flipped, preferred_element_type=jnp.float32
        )
        summed = lag_sums(product)
        begin = distance * tok_rows + 1
        totals = totals.at[:, begin : begin + 2 * tok_rows - 1].add(summed)
    partial_value = totals[:, tok_rows : tok_rows + HOPS * tok_rows]
    return lax.psum(partial_value, "ctx")


def solution(mesh):
    in_specs = (P("ctx", "ch"), P("ctx", "ch"), P("ctx", "ch"), P("ctx", "ch"))
    out_specs = P("ch", None)
    return jax.shard_map(
        on_device, mesh=mesh, in_specs=in_specs, out_specs=out_specs, check_vma=False
    )
```

profile of v0, /device:TPU:8, one launch (start us, length us, event | category | flops | bytes accessed | tf_op | source)
XLA Modules:
  0.0 446.7 jit_solution(9498662420436601433)
XLA Ops:
  0.0 1.9 multiply_convert_fusion
  1.9 0.0 copy-start
  1.9 0.0 copy-start.1
  2.0 2.9 collective-permute-start
  4.8 1.4 collective-permute-done
  6.2 14.8 %collective-permute-start.1 = (bf16[256,2048]{1,0:T(8,128)(2,1)}, bf16[256,2048]{1,0:T(8,128)(2,1)}, u32[]{:S(2)}, u32[]{:S(2)}) collective-permute-start(bf16[256,2048]{1,0:T(8,128)(2,1)} %collective-permute-done), channel_id=1, source_target_pairs={{0,2},{2,4},{4,6},{6,8},{8,10},{10,12},{12,14},{14,16},{16,18},{18... | collective-permute-start | bytes 3145736 | tf_op jit(solution)/shard_map/ppermute | solution.py:13
  21.1 10.3 %rev.15 = bf16[256,2048]{1,0:T(8,128)(2,1)} reverse(bf16[256,2048]{1,0:T(8,128)(2,1)S(1)} %multiply_convert_fusion), dimensions={0} | reverse | bytes 2097152 | tf_op jit(solution)/shard_map/rev | solution.py:35
  31.4 0.0 copy-done
  31.4 0.0 copy-done.1
  31.4 0.4 multiply_convert_fusion.1
  31.8 0.0 collective-permute-done.1
  31.8 7.3 %collective-permute-start.2 = (bf16[256,2048]{1,0:T(8,128)(2,1)}, bf16[256,2048]{1,0:T(8,128)(2,1)}, u32[]{:S(2)}, u32[]{:S(2)}) collective-permute-start(bf16[256,2048]{1,0:T(8,128)(2,1)} %collective-permute-done.1), channel_id=1, source_target_pairs={{0,2},{2,4},{4,6},{6,8},{8,10},{10,12},{12,14},{14,16},{16,18},{18... | collective-permute-start | bytes 3145736 | tf_op jit(solution)/shard_map/ppermute | solution.py:13
  39.1 0.5 fusion.12
  39.5 0.1 pad_bitcast_fusion.4
  39.7 0.8 copy.31
  40.5 0.1 slice.120
  40.6 1.2 reshape.169
  41.8 0.1 reduce_sum.45
  41.9 0.6 compare_reduce_fusion.3
  42.5 0.6 broadcast_select_fusion
  43.2 0.1 scatter-add.16
  43.3 0.6 compare_reduce_fusion.2
  43.9 0.6 compare_reduce_fusion.1
  44.6 0.7 compare_reduce_fusion
  45.2 12.7 %rev.16 = bf16[256,2048]{1,0:T(8,128)(2,1)S(1)} reverse(bf16[256,2048]{1,0:T(8,128)(2,1)} %collective-permute-done), dimensions={0} | reverse | bytes 2097152 | tf_op jit(solution)/shard_map/rev | solution.py:35
  57.9 0.5 fusion.9
  58.4 0.1 pad_bitcast_fusion.3
  58.5 0.8 copy.32
  59.4 0.1 slice.121
  59.4 1.2 reshape.172
  60.7 0.1 reduce_sum.46
  60.8 0.7 add_select_fusion.2
  61.4 0.4 scatter-add.19
  61.8 12.6 %rev.17 = bf16[256,2048]{1,0:T(8,128)(2,1)S(1)} reverse(bf16[256,2048]{1,0:T(8,128)(2,1)} %collective-permute-done.1), dimensions={0} | reverse | bytes 2097152 | tf_op jit(solution)/shard_map/rev | solution.py:35
  74.4 0.0 collective-permute-done.2
  74.5 6.0 %collective-permute-start.3 = (bf16[256,2048]{1,0:T(8,128)(2,1)}, bf16[256,2048]{1,0:T(8,128)(2,1)}, u32[]{:S(2)}, u32[]{:S(2)}) collective-permute-start(bf16[256,2048]{1,0:T(8,128)(2,1)} %collective-permute-done.2), channel_id=1, source_target_pairs={{0,2},{2,4},{4,6},{6,8},{8,10},{10,12},{12,14},{14,16},{16,18},{18... | collective-permute-start | bytes 3145736 | tf_op jit(solution)/shard_map/ppermute | solution.py:13
  80.4 0.5 fusion.6
  80.9 0.1 pad_bitcast_fusion.2
  81.0 0.8 copy.33
  81.8 0.1 slice.123
  81.9 1.2 reshape.175
  83.2 0.1 reduce_sum.47
  83.2 0.7 add_select_fusion.1
  83.9 0.3 scatter-add.20
  84.3 12.6 %rev.18 = bf16[256,2048]{1,0:T(8,128)(2,1)S(1)} reverse(bf16[256,2048]{1,0:T(8,128)(2,1)} %collective-permute-done.2), dimensions={0} | reverse | bytes 2097152 | tf_op jit(solution)/shard_map/rev | solution.py:35
  96.9 0.5 fusion.3
  97.4 0.1 pad_bitcast_fusion.1
  97.5 0.8 copy.34
  98.3 0.1 slice.125
  98.4 1.2 reshape.178
  99.6 0.1 reduce_sum.48
  99.7 0.7 add_select_fusion
  100.4 0.3 scatter-add.21
  100.7 0.0 collective-permute-done.3
  100.7 12.6 %rev.19 = bf16[256,2048]{1,0:T(8,128)(2,1)S(1)} reverse(bf16[256,2048]{1,0:T(8,128)(2,1)} %collective-permute-done.3), dimensions={0} | reverse | bytes 2097152 | tf_op jit(solution)/shard_map/rev | solution.py:35
  113.4 0.5 fusion
  113.8 0.1 pad_bitcast_fusion
  114.0 0.8 copy.35
  114.8 0.1 slice.127
  114.9 1.2 reshape.181
  116.1 0.1 reduce_sum.49
  116.2 0.1 slice_add_fusion
  116.3 0.3 scatter-add.24
  116.6 330.1 %psum.7 = f32[2,1024]{1,0:T(2,128)} all-reduce(f32[2,1024]{1,0:T(2,128)S(1)} %slice.128), channel_id=1, replica_groups=mesh['ctx'=128,'ch'=2] {'ctx'}, use_global_device_ids=true, to_apply=%region_9.10 | all-reduce | flops 2048 | bytes 16384 | tf_op jit(solution)/shard_map/psum | solution.py:43
  (7 shorter events, 0.0 us)
Async XLA Ops:
  1.9 29.4 %copy-start = (bf16[256,2048]{1,0:T(8,128)(2,1)S(1)}, bf16[256,2048]{1,0:T(8,128)(2,1)}, u32[]{:S(2)}) copy-start(bf16[256,2048]{1,0:T(8,128)(2,1)} %param.17) | copy-start | bytes 3145732
  1.9 29.4 %copy-start.1 = (bf16[256,2048]{1,0:T(8,128)(2,1)S(1)}, bf16[256,2048]{1,0:T(8,128)(2,1)}, u32[]{:S(2)}) copy-start(bf16[256,2048]{1,0:T(8,128)(2,1)} %param.14) | copy-start | bytes 3145732
  2.0 4.3 collective-permute-start
  6.2 25.5 %collective-permute-start.1 = (bf16[256,2048]{1,0:T(8,128)(2,1)}, bf16[256,2048]{1,0:T(8,128)(2,1)}, u32[]{:S(2)}, u32[]{:S(2)}) collective-permute-start(bf16[256,2048]{1,0:T(8,128)(2,1)} %collective-permute-done), channel_id=1, source_target_pairs={{0,2},{2,4},{4,6},{6,8},{8,10},{10,12},{12,14},{14,16},{16,18},{18... | collective-permute-start | bytes 3145736 | tf_op jit(solution)/shard_map/ppermute | solution.py:13
  31.4 7.7 %copy-start.4 = (bf16[256,2048]{1,0:T(8,128)(2,1)S(1)}, bf16[256,2048]{1,0:T(8,128)(2,1)}, u32[]{:S(2)}) copy-start(bf16[256,2048]{1,0:T(8,128)(2,1)} %rev.15) | copy-start | bytes 3145732
  31.8 7.3 %copy-start.2 = (bf16[256,2048]{1,0:T(8,128)(2,1)}, bf16[256,2048]{1,0:T(8,128)(2,1)S(1)}, u32[]{:S(2)}) copy-start(bf16[256,2048]{1,0:T(8,128)(2,1)S(1)} %multiply_convert_fusion.1) | copy-start | bytes 3145732
  31.8 42.7 %collective-permute-start.2 = (bf16[256,2048]{1,0:T(8,128)(2,1)}, bf16[256,2048]{1,0:T(8,128)(2,1)}, u32[]{:S(2)}, u32[]{:S(2)}) collective-permute-start(bf16[256,2048]{1,0:T(8,128)(2,1)} %collective-permute-done.1), channel_id=1, source_target_pairs={{0,2},{2,4},{4,6},{6,8},{8,10},{10,12},{12,14},{14,16},{16,18},{18... | collective-permute-start | bytes 3145736 | tf_op jit(solution)/shard_map/ppermute | solution.py:13
  45.2 12.7 %copy-start.3 = (bf16[256,2048]{1,0:T(8,128)(2,1)S(1)}, bf16[256,2048]{1,0:T(8,128)(2,1)}, u32[]{:S(2)}) copy-start(bf16[256,2048]{1,0:T(8,128)(2,1)} %copy-done.2) | copy-start | bytes 3145732
  74.5 26.3 %collective-permute-start.3 = (bf16[256,2048]{1,0:T(8,128)(2,1)}, bf16[256,2048]{1,0:T(8,128)(2,1)}, u32[]{:S(2)}, u32[]{:S(2)}) collective-permute-start(bf16[256,2048]{1,0:T(8,128)(2,1)} %collective-permute-done.2), channel_id=1, source_target_pairs={{0,2},{2,4},{4,6},{6,8},{8,10},{10,12},{12,14},{14,16},{16,18},{18... | collective-permute-start | bytes 3145736 | tf_op jit(solution)/shard_map/ppermute | solution.py:13
where the time goes:
time: 451 us; the launch traced here: 447 us
  blocking collectives  330 us (73%)
  local copies, waits for them, and re-layouts  73.4 us (16%)
  starting transfers between devices  31 us (7%)
  other arithmetic  8.06 us (2%)
    psum x1, blocking collectives, on_device(): return lax.psum(partial_value, 'ctx')  330 us
    rev x5, local copies, waits for them, and re-layouts, on_device(): flipped = blocks[distance][::-1].reshape(tok_rows, groups_here, GROUP_CH)  60.8 us
    ppermute x4, starting transfers between devices, from_behind(): return lax.ppermute(shard, axis, pairs)  31 us
  transfers between devices with their start and end apart: 4, of which 1 were waited for; matrix products, arithmetic and copies ran while one was open for 15% of the time, Pallas kernels for 0%

commit v1 on v0

--- a/solution.py
+++ b/solution.py
@@ -40,7 +40,7 @@
         begin = distance * tok_rows + 1
         totals = totals.at[:, begin : begin + 2 * tok_rows - 1].add(summed)
     partial_value = totals[:, tok_rows : tok_rows + HOPS * tok_rows]
-    return lax.psum(partial_value, "ctx")
+    return jax.lax.all_gather(partial_value, "ctx").sum(axis=0)
 
 
 def solution(mesh):

time: 451 us -> 246 us (0.55)
  the two profiles are of different devices: /device:TPU:8 before, /device:TPU:1 now
where the time goes in v1:
time: 246 us; the launch traced here: 242 us
  waiting for transfers between devices  121 us (49%)
  local copies, waits for them, and re-layouts  74 us (30%)
  starting transfers between devices  20.3 us (8%)
  between operations  13.8 us (6%)
  other arithmetic  10.2 us (4%)
    all_gather x1, waiting for transfers between devices, on_device(): return jax.lax.all_gather(partial_value, 'ctx').sum(axis=0)  108 us
    rev x5, local copies, waits for them, and re-layouts, on_device(): flipped = blocks[distance][::-1].reshape(tok_rows, groups_here, GROUP_CH)  60.8 us
    ppermute x4, starting transfers between devices, from_behind(): return lax.ppermute(shard, axis, pairs)  20.3 us
    ppermute x4, waiting for transfers between devices, from_behind(): return lax.ppermute(shard, axis, pairs)  13.1 us
    reshape x5, local copies, waits for them, and re-layouts, lag_sums(): return jnp.sum(flat.reshape(count, tok_rows, 2 * tok_rows - 1), axis=1)  6.16 us
    unnamed x21, local copies, waits for them, and re-layouts  5.29 us
    another operation x8, other arithmetic  5.26 us
  transfers between devices with their start and end apart: 5, of which 3 were waited for; matrix products, arithmetic and copies ran while one was open for 27% of the time, Pallas kernels for 0%

profile of v1, /device:TPU:1, one launch (start us, length us, event | category | flops | bytes accessed | tf_op | source)
XLA Modules:
  0.0 241.6 jit_solution(14428941229039422685)
XLA Ops:
  6.5 1.9 multiply_convert_fusion
  8.5 0.0 copy-start
  8.5 0.0 copy-start.1
  8.5 6.3 %collective-permute-start = (bf16[256,2048]{1,0:T(8,128)(2,1)S(1)}, bf16[256,2048]{1,0:T(8,128)(2,1)}, u32[]{:S(2)}, u32[]{:S(2)}) collective-permute-start(bf16[256,2048]{1,0:T(8,128)(2,1)S(1)} %multiply_convert_fusion), channel_id=1, source_target_pairs={{0,2},{2,4},{4,6},{6,8},{8,10},{10,12},{12,14},{14,16},{16,18},{18... | collective-permute-start | bytes 3145736 | tf_op jit(solution)/shard_map/ppermute | solution.py:13
  14.9 11.7 %collective-permute-done = bf16[256,2048]{1,0:T(8,128)(2,1)} collective-permute-done((bf16[256,2048]{1,0:T(8,128)(2,1)S(1)}, bf16[256,2048]{1,0:T(8,128)(2,1)}, u32[]{:S(2)}, u32[]{:S(2)}) %collective-permute-start) | collective-permute-done | bytes 1048608 | tf_op jit(solution)/shard_map/ppermute | solution.py:13
  26.6 6.0 %collective-permute-start.1 = (bf16[256,2048]{1,0:T(8,128)(2,1)}, bf16[256,2048]{1,0:T(8,128)(2,1)}, u32[]{:S(2)}, u32[]{:S(2)}) collective-permute-start(bf16[256,2048]{1,0:T(8,128)(2,1)} %collective-permute-done), channel_id=1, source_target_pairs={{0,2},{2,4},{4,6},{6,8},{8,10},{10,12},{12,14},{14,16},{16,18},{18... | collective-permute-start | bytes 3145736 | tf_op jit(solution)/shard_map/ppermute | solution.py:13
  32.6 10.3 %rev.15 = bf16[256,2048]{1,0:T(8,128)(2,1)} reverse(bf16[256,2048]{1,0:T(8,128)(2,1)S(1)} %multiply_convert_fusion), dimensions={0} | reverse | bytes 2097152 | tf_op jit(solution)/shard_map/rev | solution.py:35
  42.9 0.4 multiply_convert_fusion.1
  43.3 1.3 collective-permute-done.1
  44.6 5.9 %collective-permute-start.2 = (bf16[256,2048]{1,0:T(8,128)(2,1)}, bf16[256,2048]{1,0:T(8,128)(2,1)}, u32[]{:S(2)}, u32[]{:S(2)}) collective-permute-start(bf16[256,2048]{1,0:T(8,128)(2,1)} %collective-permute-done.1), channel_id=1, source_target_pairs={{0,2},{2,4},{4,6},{6,8},{8,10},{10,12},{12,14},{14,16},{16,18},{18... | collective-permute-start | bytes 3145736 | tf_op jit(solution)/shard_map/ppermute | solution.py:13
  50.5 0.5 fusion.12
  51.0 0.1 pad_bitcast_fusion.4
  51.1 0.8 copy.41
  51.9 0.1 slice.120
  52.0 1.2 reshape.169
  53.3 0.1 reduce_sum.54
  53.3 0.6 compare_reduce_fusion.3
  54.0 0.6 broadcast_select_fusion
  54.6 0.1 scatter-add.16
  54.7 0.6 compare_reduce_fusion.2
  55.4 0.6 compare_reduce_fusion.1
  56.0 0.7 compare_reduce_fusion
  56.7 12.7 %rev.16 = bf16[256,2048]{1,0:T(8,128)(2,1)S(1)} reverse(bf16[256,2048]{1,0:T(8,128)(2,1)} %collective-permute-done), dimensions={0} | reverse | bytes 2097152 | tf_op jit(solution)/shard_map/rev | solution.py:35
  69.4 0.5 fusion.9
  69.9 0.1 pad_bitcast_fusion.3
  70.0 0.8 copy.42
  70.8 0.1 slice.121
  70.9 1.2 reshape.172
  72.1 0.1 reduce_sum.55
  72.2 0.7 add_select_fusion.2
  72.9 0.4 scatter-add.19
  73.3 12.6 %rev.17 = bf16[256,2048]{1,0:T(8,128)(2,1)S(1)} reverse(bf16[256,2048]{1,0:T(8,128)(2,1)} %collective-permute-done.1), dimensions={0} | reverse | bytes 2097152 | tf_op jit(solution)/shard_map/rev | solution.py:35
  85.9 0.0 collective-permute-done.2
  85.9 2.1 collective-permute-start.3
  88.0 0.5 fusion.6
  88.5 0.1 pad_bitcast_fusion.2
  88.6 0.8 copy.43
  89.4 0.1 slice.123
  89.5 1.2 reshape.175
  90.8 0.1 reduce_sum.56
  90.8 0.7 add_select_fusion.1
  91.5 0.3 scatter-add.20
  91.9 12.6 %rev.18 = bf16[256,2048]{1,0:T(8,128)(2,1)S(1)} reverse(bf16[256,2048]{1,0:T(8,128)(2,1)} %collective-permute-done.2), dimensions={0} | reverse | bytes 2097152 | tf_op jit(solution)/shard_map/rev | solution.py:35
  104.5 0.5 fusion.3
  105.0 0.1 pad_bitcast_fusion.1
  105.1 0.8 copy.44
  105.9 0.1 slice.125
  106.0 1.2 reshape.178
  107.2 0.1 reduce_sum.57
  107.3 0.7 add_select_fusion
  108.0 0.3 scatter-add.21
  108.3 12.6 %rev.19 = bf16[256,2048]{1,0:T(8,128)(2,1)S(1)} reverse(bf16[256,2048]{1,0:T(8,128)(2,1)} %collective-permute-done.3), dimensions={0} | reverse | bytes 2097152 | tf_op jit(solution)/shard_map/rev | solution.py:35
  120.9 0.5 fusion
  121.4 0.1 pad_bitcast_fusion
  121.5 0.8 copy.45
  122.4 0.1 slice.127
  122.4 1.2 reshape.181
  123.7 0.1 reduce_sum.58
  123.8 0.1 slice_add_fusion
  123.8 0.3 scatter-add.24
  124.1 0.6 slice_bitcast_fusion
  124.7 0.0 all-gather.4.cloned.1.call-update
  124.8 107.8 %all-gather.4.cloned.1.call-done = f32[128,2,1024]{2,1,0:T(2,128)} async-done(((f32[1,2,1024]{2,1,0:T(2,128)}), f32[128,2,1024]{2,1,0:T(2,128)}) %all-gather.4.cloned.1.call-update) | async-done | bytes 1048592 | tf_op jit(solution)/shard_map/all_gather | solution.py:43
  232.6 2.2 reduce_sum.59
  (10 shorter events, 0.0 us)
Async XLA Ops:
  6.5 226.0 %all-gather.4.cloned.1.call-start = ((), (), s32[]{:S(2)}) async-start(), calls=%async_computation | async-start | bytes 1056768 | tf_op jit(solution)/shard_map/all_gather | solution.py:43
  8.5 34.4 %copy-start = (bf16[256,2048]{1,0:T(8,128)(2,1)S(1)}, bf16[256,2048]{1,0:T(8,128)(2,1)}, u32[]{:S(2)}) copy-start(bf16[256,2048]{1,0:T(8,128)(2,1)} %param.17) | copy-start | bytes 3145732
  8.5 34.4 %copy-start.1 = (bf16[256,2048]{1,0:T(8,128)(2,1)S(1)}, bf16[256,2048]{1,0:T(8,128)(2,1)}, u32[]{:S(2)}) copy-start(bf16[256,2048]{1,0:T(8,128)(2,1)} %param.14) | copy-start | bytes 3145732
  8.5 18.1 %collective-permute-start = (bf16[256,2048]{1,0:T(8,128)(2,1)S(1)}, bf16[256,2048]{1,0:T(8,128)(2,1)}, u32[]{:S(2)}, u32[]{:S(2)}) collective-permute-start(bf16[256,2048]{1,0:T(8,128)(2,1)S(1)} %multiply_convert_fusion), channel_id=1, source_target_pairs={{0,2},{2,4},{4,6},{6,8},{8,10},{10,12},{12,14},{14,16},{16,18},{18... | collective-permute-start | bytes 3145736 | tf_op jit(solution)/shard_map/ppermute | solution.py:13
  26.6 18.0 %collective-permute-start.1 = (bf16[256,2048]{1,0:T(8,128)(2,1)}, bf16[256,2048]{1,0:T(8,128)(2,1)}, u32[]{:S(2)}, u32[]{:S(2)}) collective-permute-start(bf16[256,2048]{1,0:T(8,128)(2,1)} %collective-permute-done), channel_id=1, source_target_pairs={{0,2},{2,4},{4,6},{6,8},{8,10},{10,12},{12,14},{14,16},{16,18},{18... | collective-permute-start | bytes 3145736 | tf_op jit(solution)/shard_map/ppermute | solution.py:13
  42.9 7.6 %copy-start.4 = (bf16[256,2048]{1,0:T(8,128)(2,1)S(1)}, bf16[256,2048]{1,0:T(8,128)(2,1)}, u32[]{:S(2)}) copy-start(bf16[256,2048]{1,0:T(8,128)(2,1)} %rev.15) | copy-start | bytes 3145732
  43.3 7.2 %copy-start.2 = (bf16[256,2048]{1,0:T(8,128)(2,1)}, bf16[256,2048]{1,0:T(8,128)(2,1)S(1)}, u32[]{:S(2)}) copy-start(bf16[256,2048]{1,0:T(8,128)(2,1)S(1)} %multiply_convert_fusion.1) | copy-start | bytes 3145732
  44.6 41.3 %collective-permute-start.2 = (bf16[256,2048]{1,0:T(8,128)(2,1)}, bf16[256,2048]{1,0:T(8,128)(2,1)}, u32[]{:S(2)}, u32[]{:S(2)}) collective-permute-start(bf16[256,2048]{1,0:T(8,128)(2,1)} %collective-permute-done.1), channel_id=1, source_target_pairs={{0,2},{2,4},{4,6},{6,8},{8,10},{10,12},{12,14},{14,16},{16,18},{18... | collective-permute-start | bytes 3145736 | tf_op jit(solution)/shard_map/ppermute | solution.py:13
  56.7 12.7 %copy-start.3 = (bf16[256,2048]{1,0:T(8,128)(2,1)S(1)}, bf16[256,2048]{1,0:T(8,128)(2,1)}, u32[]{:S(2)}) copy-start(bf16[256,2048]{1,0:T(8,128)(2,1)} %copy-done.2) | copy-start | bytes 3145732
  85.9 22.4 %collective-permute-start.3 = (bf16[256,2048]{1,0:T(8,128)(2,1)}, bf16[256,2048]{1,0:T(8,128)(2,1)}, u32[]{:S(2)}, u32[]{:S(2)}) collective-permute-start(bf16[256,2048]{1,0:T(8,128)(2,1)} %collective-permute-done.2), channel_id=1, source_target_pairs={{0,2},{2,4},{4,6},{6,8},{8,10},{10,12},{12,14},{14,16},{16,18},{18... | collective-permute-start | bytes 3145736 | tf_op jit(solution)/shard_map/ppermute | solution.py:13
Sparse Core Ops, SparseCore 0:
  124.9 107.6 all-gather.3
